TPU v7x, 32 devices: a whole 2x2x4 slice. The times are simulated.
32 devices in a mesh: ep: 16 (over z, y, x), dp: 2 (over core).
Axes of the slice: x: 2, y: 2, z: 4, core: 2. Of those that a mesh axis runs over, the one named last changes fastest.
Arguments:
- tokens: bfloat16 [4096, 768], P(('ep', 'dp')), may hold values from -6 to 6
- routing: int32 [4096, 1], P(('ep', 'dp')), may hold values from 0 to 15; in each aligned block of 128 rows (0 to 127, 128 to 255, ...) at most 16 rows name the same one
- gate_prob: float32 [4096], P(('ep', 'dp')), may hold values from 0.2 to 1
- up_weight: bfloat16 [16, 768, 3072], P('ep', None, 'dp'), may hold values from -0.21875 to 0.21875
- down_weight: bfloat16 [16, 3072, 768], P('ep', 'dp'), may hold values from -0.109375 to 0.109375
- out_grad: bfloat16 [4096, 768], P(('ep', 'dp')), may hold values from -1.5 to 1.5
Outputs:
- output: bfloat16 [4096, 768], P(('ep', 'dp'))
- token_grad: bfloat16 [4096, 768], P(('ep', 'dp'))
- prob_grad: float32 [4096], P(('ep', 'dp'))
- up_grad: bfloat16 [16, 768, 3072], P('ep', None, 'dp')
- down_grad: bfloat16 [16, 3072, 768], P('ep', 'dp')
Inputs may be any that keep to these rules, and one draw needn't show every extreme that they name: `routing`: among the 128 rows of one device (devices in the order of ep, then dp) no expert is named more than 16 times; in some devices' rows some expert is named exactly 16 times; every expert is named somewhere.
All inputs are finite; a program needn't handle non-finite values.
Results may differ from a plain program's by a relative error of at most 0.0058.
Values may be sent and summed in bfloat16 or wider, within the bound.
A program may use at most 64 MiB of HBM per device.

v0:
```python
import jax
import jax.numpy as jnp
from jax import lax
from jax.sharding import PartitionSpec as P


def local(tokens, routing, gate_prob, up_weight, down_weight, out_grad):
    token_count = tokens.shape[0]
    local_experts = up_weight.shape[0]
    peer_count = lax.axis_size("ep")
    experts = local_experts * peer_count
    capacity = max(2, 2 * token_count // experts)
    slot_count = experts * capacity
    expert = routing[:, 0]
    onehot = (expert[:, None] == jnp.arange(experts, dtype=jnp.int32)[None, :]).astype(jnp.int32)
    ranking = jnp.sum((jnp.cumsum(onehot, axis=0) - onehot) * onehot, axis=1)
    target = expert * capacity + ranking
    placing = (jnp.arange(slot_count, dtype=jnp.int32)[:, None] == target[None, :]).astype(
        jnp.bfloat16
    )

    def dispatch(values):
        packed = jnp.dot(placing, values, preferred_element_type=jnp.float32).astype(jnp.bfloat16)
        return packed.reshape(experts, capacity, values.shape[1])

    def collect(returned):
        flat = returned.reshape(slot_count, returned.shape[2])
        return jnp.einsum("st,sd->td", placing, flat, preferred_element_type=jnp.float32)

    grad_wide = out_grad.astype(jnp.float32)
    scaled = (gate_prob[:, None] * grad_wide).astype(jnp.bfloat16)
    sent_rows = lax.all_to_all(dispatch(tokens), "ep", split_axis=0, concat_axis=1, tiled=True)
    expert_rows = lax.all_gather(sent_rows, "dp", axis=1, tiled=True)
    up_full, down_full = (up_weight, down_weight)
    preact = jnp.einsum("erd,edf->erf", expert_rows, up_full, preferred_element_type=jnp.float32)
    activated, back_fn = jax.vjp(jax.nn.gelu, preact)
    hidden = activated.astype(jnp.bfloat16)
    partial_out = jnp.einsum("erf,efd->erd", hidden, down_full, preferred_element_type=jnp.float32)
    merged = lax.psum_scatter(partial_out, "dp", scatter_dimension=1, tiled=True)
    expert_out = lax.all_to_all(
        merged.astype(jnp.bfloat16), "ep", split_axis=1, concat_axis=0, tiled=True
    )
    expert_tok = collect(expert_out)
    output = (gate_prob[:, None] * expert_tok).astype(jnp.bfloat16)
    prob_grad = jnp.sum(grad_wide * expert_tok, axis=1)
    sent_grads = lax.all_to_all(dispatch(scaled), "ep", split_axis=0, concat_axis=1, tiled=True)
    grad_rows = lax.all_gather(sent_grads, "dp", axis=1, tiled=True)
    hidden_grad = jnp.einsum(
        "erd,efd->erf", grad_rows, down_full, preferred_element_type=jnp.float32
    )
    preact_grad = back_fn(hidden_grad)[0].astype(jnp.bfloat16)
    partial_input = jnp.einsum(
        "erf,edf->erd", preact_grad, up_full, preferred_element_type=jnp.float32
    )
    up_sum = jnp.einsum(
        "erd,erf->edf", expert_rows, preact_grad, preferred_element_type=jnp.float32
    )
    down_sum = jnp.einsum("erf,erd->efd", hidden, grad_rows, preferred_element_type=jnp.float32)
    input_rows = lax.psum_scatter(partial_input, "dp", scatter_dimension=1, tiled=True)
    up_grad = up_sum.astype(jnp.bfloat16)
    down_grad = down_sum.astype(jnp.bfloat16)
    returned = lax.all_to_all(
        input_rows.astype(jnp.bfloat16), "ep", split_axis=1, concat_axis=0, tiled=True
    )
    token_grad = collect(returned).astype(jnp.bfloat16)
    return (output, token_grad, prob_grad, up_grad, down_grad)


def solution(mesh):
    placed = (
        P(("ep", "dp"), None),
        P(("ep", "dp"), None),
        P(("ep", "dp")),
        P("ep", None, "dp"),
        P("ep", "dp", None),
        P(("ep", "dp"), None),
    )
    return jax.shard_map(
        local,
        mesh=mesh,
        in_specs=placed,
        out_specs=(
            P(("ep", "dp"), None),
            P(("ep", "dp"), None),
            P(("ep", "dp")),
            P("ep", None, "dp"),
            P("ep", "dp", None),
        ),
        check_vma=False,
    )
```

profile of v0, /device:TPU:0, one launch (start us, length us, event | category | flops | bytes accessed | tf_op | source)
XLA Modules:
  0.0 124.0 jit_solution(15889693850818185313)
XLA Ops:
  7.2 0.0 copy-start
  7.2 0.9 fusion.42
  8.1 0.2 reduce_window_sum.11
  8.2 0.8 select_reduce_fusion
  9.1 0.7 multiply_add_fusion
  9.7 1.9 %convolution_convert_fusion.3 = bf16[256,768]{1,0:T(8,128)(2,1)} fusion(bf16[128,768]{1,0:T(8,128)(2,1)} %param.6, s32[128]{0:T(128)S(1)} %multiply_add_fusion), kind=kOutput, calls=%fused_computation.25 | convolution fusion | flops 50561024 | bytes 590336 | tf_op jit(solution)/shard_map/dot_general | solution.py:23
  11.7 8.3 %all-to-all-start = ((bf16[16,16,768]{2,1,0:T(8,128)(2,1)}), bf16[16,16,768]{2,1,0:T(8,128)(2,1)S(1)}, u32[]{:S(2)}, u32[]{:S(2)}) async-start(bf16[16,16,768]{2,1,0:T(8,128)(2,1)} %bitcast.1), calls=%async_computation | async-start | bytes 786432 | tf_op jit(solution)/shard_map/all_to_all | solution.py:32
  20.0 2.0 %convolution_convert_fusion.2 = bf16[256,768]{1,0:T(8,128)(2,1)} fusion(bf16[128,768]{1,0:T(8,128)(2,1)} %param.11, f32[128]{0:T(128)} %param.8, s32[128]{0:T(128)S(1)} %multiply_add_fusion), kind=kOutput, calls=%fused_computation.24 | convolution fusion | flops 50855936 | bytes 590848 | tf_op jit(solution)/shard_map/dot_general | solution.py:23
  22.0 10.6 %all-to-all-done = bf16[16,16,768]{2,1,0:T(8,128)(2,1)S(1)} async-done(((bf16[16,16,768]{2,1,0:T(8,128)(2,1)}), bf16[16,16,768]{2,1,0:T(8,128)(2,1)S(1)}, u32[]{:S(2)}, u32[]{:S(2)}) %all-to-all-start) | async-done | bytes 393248 | tf_op jit(solution)/shard_map/all_to_all | solution.py:32
  32.6 3.6 %all-to-all-start.2 = ((bf16[16,16,768]{2,1,0:T(8,128)(2,1)}), bf16[16,16,768]{2,1,0:T(8,128)(2,1)S(1)}, u32[]{:S(2)}, u32[]{:S(2)}) async-start(bf16[16,16,768]{2,1,0:T(8,128)(2,1)} %bitcast.7), calls=%async_computation.3 | async-start | bytes 786432 | tf_op jit(solution)/shard_map/all_to_all | solution.py:46
  36.2 0.0 reduce-scatter.5.cloned.1.call-start
  36.3 2.5 %all_gather.6 = bf16[1,512,768]{2,1,0:T(8,128)(2,1)} all-gather(bf16[1,256,768]{2,1,0:T(8,128)(2,1)S(1)} %bitcast.62), channel_id=1, replica_groups=mesh['ep'=16,'dp'=2] {'dp'}, dimensions={1}, use_global_device_ids=true | all-gather | bytes 1179648 | tf_op jit(solution)/shard_map/all_gather | solution.py:33
  38.8 9.4 %all-to-all-done.2 = bf16[16,16,768]{2,1,0:T(8,128)(2,1)S(1)} async-done(((bf16[16,16,768]{2,1,0:T(8,128)(2,1)}), bf16[16,16,768]{2,1,0:T(8,128)(2,1)S(1)}, u32[]{:S(2)}, u32[]{:S(2)}) %all-to-all-start.2) | async-done | bytes 393248 | tf_op jit(solution)/shard_map/all_to_all | solution.py:46
  48.2 2.4 %all_gather.7 = bf16[1,512,768]{2,1,0:T(8,128)(2,1)S(1)} all-gather(bf16[1,256,768]{2,1,0:T(8,128)(2,1)S(1)} %bitcast.63), channel_id=1, replica_groups=mesh['ep'=16,'dp'=2] {'dp'}, dimensions={1}, use_global_device_ids=true | all-gather | bytes 1179648 | tf_op jit(solution)/shard_map/all_gather | solution.py:47
  50.6 0.0 copy-done
  50.6 2.9 %fusion.17 = f32[512,1536]{1,0:T(8,128)S(1)} fusion(bf16[1,768,1536]{2,1,0:T(8,128)(2,1)S(1)} %copy-done, bf16[1,512,768]{2,1,0:T(8,128)(2,1)} %all_gather.6), kind=kOutput, calls=%fused_computation.20 | convolution fusion | flops 1207959552 | bytes 6291456 | tf_op jit(solution)/shard_map/erd,edf->erf/dot_general | solution.py:35
  53.4 0.0 copy-done.1
  53.4 0.0 copy-done.3
  53.5 0.0 copy-start.4
  53.5 3.0 %fusion.6 = bf16[512,1536]{1,0:T(8,128)(2,1)S(1)} fusion(f32[512,1536]{1,0:T(8,128)S(1)} %fusion.17, bf16[1,1536,768]{2,1,0:T(8,128)(2,1)S(1)} %copy-done.3, bf16[1,512,768]{2,1,0:T(8,128)(2,1)S(1)} %all_gather.7), kind=kOutput, calls=%fused_computation.10 | convolution fusion | flops 1223688192 | bytes 7864320 | tf_op jit(solution)/shard_map/erd,efd->erf/dot_general | solution.py:48
  56.5 1.1 copy-done.5
  57.7 2.6 %fusion.19 = f32[1,512,768]{2,1,0:T(8,128)} fusion(bf16[512,1536]{1,0:T(8,128)(2,1)S(1)} %fusion.6, bf16[1,768,1536]{2,1,0:T(8,128)(2,1)S(1)} %copy-done), kind=kOutput, calls=%fused_computation.22 | convolution fusion | flops 1207959552 | bytes 5505024 | tf_op jit(solution)/shard_map/erf,edf->erd/dot_general | solution.py:52
  60.2 0.0 reduce-scatter.5.cloned.1.call-update
  60.2 0.0 reduce-scatter.3.cloned.1.call-start
  60.3 5.7 %fusion.22 = f32[1,512,768]{2,1,0:T(8,128)} fusion(bf16[1,1536,768]{2,1,0:T(8,128)(2,1)} %param.10, f32[512,1536]{1,0:T(8,128)} %copy-done.4), kind=kOutput, calls=%fused_computation.23 | convolution fusion | flops 1215037440 | bytes 7077888 | tf_op jit(solution)/shard_map/erf,efd->erd/dot_general | solution.py:38
  66.0 0.0 reduce-scatter.3.cloned.1.call-update
  66.0 1.4 %reduce-scatter.5.cloned.1.call-done = f32[1,256,768]{2,1,0:T(8,128)} async-done(((f32[1,512,768]{2,1,0:T(8,128)}), f32[1,256,768]{2,1,0:T(8,128)}) %reduce-scatter.5.cloned.1.call-update) | async-done | bytes 786448 | tf_op jit(solution)/shard_map/reduce_scatter | solution.py:59
  67.5 1.2 convert_element_type.57
  68.7 0.6 copy.29
  69.3 0.5 broadcast.52
  69.8 3.0 %reduce.1 = bf16[256,768]{1,0:T(8,128)(2,1)S(1)} reduce(bf16[256,1,768]{2,1,0:T(2,128)(2,1)S(1)} %bitcast.59, bf16[]{:T(256)} %broadcast.52), dimensions={1}, to_apply=%bitcast.57.reduce_sub_computation | reduce | bytes 786434
  72.8 0.9 reshape.110
  73.7 6.8 %all-to-all-start.3 = ((bf16[16,2,6144]{2,1,0:T(2,128)(2,1)}), bf16[16,2,6144]{2,1,0:T(2,128)(2,1)S(1)}, u32[]{:S(2)}, u32[]{:S(2)}) async-start(bf16[16,2,6144]{2,1,0:T(2,128)(2,1)} %reshape.110), calls=%async_computation.5 | async-start | bytes 786432 | tf_op jit(solution)/shard_map/all_to_all | solution.py:62
  80.5 4.5 %fusion.7 = bf16[1,768,1536]{2,1,0:T(8,128)(2,1)} fusion(bf16[512,1536]{1,0:T(8,128)(2,1)} %copy-done.5, bf16[1,512,768]{2,1,0:T(8,128)(2,1)} %all_gather.6), kind=kOutput, calls=%fused_computation.12 | convolution fusion | flops 1209139200 | bytes 4718592 | tf_op jit(solution)/shard_map/erd,erf->edf/dot_general | solution.py:55
  85.0 1.2 convert_element_type.51
  86.2 0.6 copy.30
  86.8 3.8 %reduce = bf16[256,768]{1,0:T(8,128)(2,1)} reduce(bf16[256,1,768]{2,1,0:T(2,128)(2,1)S(1)} %bitcast.60, bf16[]{:T(256)} %broadcast.52), dimensions={1}, to_apply=%bitcast.58.reduce_sub_computation | reduce | bytes 786434
  90.5 1.8 %reshape.108 = bf16[16,2,6144]{2,1,0:T(2,128)(2,1)} reshape(bf16[256,768]{1,0:T(8,128)(2,1)} %reduce) | data formatting | bytes 786432
  92.4 1.2 all-to-all-done.3
  93.5 5.8 %all-to-all-start.1 = ((bf16[16,2,6144]{2,1,0:T(2,128)(2,1)}), bf16[16,2,6144]{2,1,0:T(2,128)(2,1)}, u32[]{:S(2)}, u32[]{:S(2)}) async-start(bf16[16,2,6144]{2,1,0:T(2,128)(2,1)} %reshape.108), calls=%async_computation.2 | async-start | bytes 786432 | tf_op jit(solution)/shard_map/all_to_all | solution.py:40
  99.3 0.0 copy-start.2
  99.3 5.2 %fusion.8 = bf16[1,1536,768]{2,1,0:T(8,128)(2,1)} fusion(bf16[1,512,768]{2,1,0:T(8,128)(2,1)} %copy-done.1, f32[512,1536]{1,0:T(8,128)} %copy-done.4), kind=kOutput, calls=%fused_computation.13 | convolution fusion | flops 1216217088 | bytes 6291456 | tf_op jit(solution)/shard_map/erf,erd->efd/dot_general | solution.py:58
  104.6 0.4 reshape.111
  104.9 0.9 convolution_convert_fusion.4
  105.9 6.1 %all-to-all-done.1 = bf16[16,2,6144]{2,1,0:T(2,128)(2,1)} async-done(((bf16[16,2,6144]{2,1,0:T(2,128)(2,1)}), bf16[16,2,6144]{2,1,0:T(2,128)(2,1)}, u32[]{:S(2)}, u32[]{:S(2)}) %all-to-all-start.1) | async-done | bytes 393248 | tf_op jit(solution)/shard_map/all_to_all | solution.py:40
  112.0 2.7 %reshape.109 = bf16[256,1,768]{2,1,0:T(2,128)(2,1)S(1)} reshape(bf16[16,2,6144]{2,1,0:T(2,128)(2,1)} %all-to-all-done.1) | data formatting | bytes 786432
  114.7 0.0 copy-done.2
  114.7 2.5 %fusion.30 = (f32[128]{0:T(128)}, bf16[128,768]{1,0:T(8,128)(2,1)}) fusion(bf16[128,768]{1,0:T(8,128)(2,1)} %param.11, f32[128]{0:T(128)S(1)} %copy-done.2, bf16[1,256,768]{2,0,1:T(2,128)(2,1)S(1)} %bitcast.64, s32[128]{0:T(128)S(1)} %multiply_add_fusion), kind=kOutput, calls=%fused_computation.34 | convolution fusion | flops 50855808 | bytes 787968 | tf_op jit(solution)/shard_map/st,sd->td/dot_general | solution.py:28
  (5 shorter events, 0.0 us)
Async XLA Ops:
  7.2 43.4 %copy-start = (bf16[1,768,1536]{2,1,0:T(8,128)(2,1)S(1)}, bf16[1,768,1536]{2,1,0:T(8,128)(2,1)}, u32[]{:S(2)}) copy-start(bf16[1,768,1536]{2,1,0:T(8,128)(2,1)} %param.9) | copy-start | bytes 7077892
  11.7 21.0 %all-to-all-start = ((bf16[16,16,768]{2,1,0:T(8,128)(2,1)}), bf16[16,16,768]{2,1,0:T(8,128)(2,1)S(1)}, u32[]{:S(2)}, u32[]{:S(2)}) async-start(bf16[16,16,768]{2,1,0:T(8,128)(2,1)} %bitcast.1), calls=%async_computation | async-start | bytes 786432 | tf_op jit(solution)/shard_map/all_to_all | solution.py:32
  32.6 15.6 %all-to-all-start.2 = ((bf16[16,16,768]{2,1,0:T(8,128)(2,1)}), bf16[16,16,768]{2,1,0:T(8,128)(2,1)S(1)}, u32[]{:S(2)}, u32[]{:S(2)}) async-start(bf16[16,16,768]{2,1,0:T(8,128)(2,1)} %bitcast.7), calls=%async_computation.3 | async-start | bytes 786432 | tf_op jit(solution)/shard_map/all_to_all | solution.py:46
  36.2 31.3 %reduce-scatter.5.cloned.1.call-start = ((), (), s32[]{:S(2)}) async-start(), calls=%async_computation.7 | async-start | bytes 2359296 | tf_op jit(solution)/shard_map/reduce_scatter | solution.py:59
  50.6 2.9 %copy-start.1 = (bf16[1,512,768]{2,1,0:T(8,128)(2,1)}, bf16[1,512,768]{2,1,0:T(8,128)(2,1)S(1)}, u32[]{:S(2)}) copy-start(bf16[1,512,768]{2,1,0:T(8,128)(2,1)S(1)} %all_gather.7) | copy-start | bytes 2359300
  50.6 2.9 %copy-start.3 = (bf16[1,1536,768]{2,1,0:T(8,128)(2,1)S(1)}, bf16[1,1536,768]{2,1,0:T(8,128)(2,1)}, u32[]{:S(2)}) copy-start(bf16[1,1536,768]{2,1,0:T(8,128)(2,1)} %param.10) | copy-start | bytes 7077892
  53.5 3.1 %copy-start.4 = (f32[512,1536]{1,0:T(8,128)}, f32[512,1536]{1,0:T(8,128)S(1)}, u32[]{:S(2)}) copy-start(f32[512,1536]{1,0:T(8,128)S(1)} %fusion.17) | copy-start | bytes 9437188
  56.5 1.2 copy-start.5
  60.2 24.7 %reduce-scatter.3.cloned.1.call-start = ((), (), s32[]{:S(2)}) async-start(), calls=%async_computation.6 | async-start | bytes 2359296 | tf_op jit(solution)/shard_map/reduce_scatter | solution.py:39
  73.7 19.9 %all-to-all-start.3 = ((bf16[16,2,6144]{2,1,0:T(2,128)(2,1)}), bf16[16,2,6144]{2,1,0:T(2,128)(2,1)S(1)}, u32[]{:S(2)}, u32[]{:S(2)}) async-start(bf16[16,2,6144]{2,1,0:T(2,128)(2,1)} %reshape.110), calls=%async_computation.5 | async-start | bytes 786432 | tf_op jit(solution)/shard_map/all_to_all | solution.py:62
  93.5 18.4 %all-to-all-start.1 = ((bf16[16,2,6144]{2,1,0:T(2,128)(2,1)}), bf16[16,2,6144]{2,1,0:T(2,128)(2,1)}, u32[]{:S(2)}, u32[]{:S(2)}) async-start(bf16[16,2,6144]{2,1,0:T(2,128)(2,1)} %reshape.108), calls=%async_computation.2 | async-start | bytes 786432 | tf_op jit(solution)/shard_map/all_to_all | solution.py:40
  99.3 15.4 %copy-start.2 = (f32[128]{0:T(128)S(1)}, f32[128]{0:T(128)}, u32[]{:S(2)}) copy-start(f32[128]{0:T(128)} %param.8) | copy-start | bytes 1540
Sparse Core Ops, SparseCore 0:
  60.4 7.0 reduce-scatter.4
  70.4 10.2 reduce-scatter.2
where the time goes:
time: 125 us; the launch traced here: 124 us
  matrix products  31.2 us (25%)
  waiting for transfers between devices  28.8 us (23%)
  starting transfers between devices  24.6 us (20%)
  between operations  14.2 us (11%)
  other arithmetic  11.7 us (9%)
  local copies, waits for them, and re-layouts  8.7 us (7%)
  blocking collectives  4.86 us (4%)
    all_to_all x1, waiting for transfers between devices, local(): lax.all_to_all(dispatch(tokens), 'ep', split_axis=0, concat_axis=1, tiled...  10.6 us
    all_to_all x1, waiting for transfers between devices, local(): lax.all_to_all(dispatch(scaled), 'ep', split_axis=0, concat_axis=1, tiled...  9.45 us
    all_to_all x1, starting transfers between devices, local(): lax.all_to_all(dispatch(tokens), 'ep', split_axis=0, concat_axis=1, tiled...  8.31 us
    unnamed x17, local copies, waits for them, and re-layouts  7.49 us
    all_to_all x1, starting transfers between devices, local(): lax.all_to_all(input_rows.astype(jnp.bfloat16), 'ep', split_axis=1, conca...  6.84 us
    unnamed x2, other arithmetic  6.76 us
    all_to_all x1, waiting for transfers between devices, local(): lax.all_to_all(merged.astype(jnp.bfloat16), 'ep', split_axis=1, concat_ax...  6.08 us
    all_to_all x1, starting transfers between devices, local(): lax.all_to_all(merged.astype(jnp.bfloat16), 'ep', split_axis=1, concat_ax...  5.79 us
  transfers between devices with their start and end apart: 6, of which 5 were waited for; matrix products, arithmetic and copies ran while one was open for 26% of the time, Pallas kernels for 0%

commit v1 on v0

--- a/solution.py
+++ b/solution.py
@@ -1,10 +1,14 @@
+import functools
+
 import jax
 import jax.numpy as jnp
 from jax import lax
+from jax.experimental import pallas as pl
+from jax.experimental.pallas import tpu as pltpu
 from jax.sharding import PartitionSpec as P
 
 
-def local(tokens, routing, gate_prob, up_weight, down_weight, out_grad):
+def local_plain(tokens, routing, gate_prob, up_weight, down_weight, out_grad):
     token_count = tokens.shape[0]
     local_experts = up_weight.shape[0]
     peer_count = lax.axis_size("ep")
@@ -66,6 +70,362 @@
     return (output, token_grad, prob_grad, up_grad, down_grad)
 
 
+MESH = pl.DeviceIdType.MESH
+TILE = 16
+CHUNK = 256
+SCALE = 0.7978845608028654
+CUBIC = 0.044715
+
+
+def row_block(start, size):
+    return pl.ds(pl.multiple_of(start, TILE), size)
+
+
+def kernel(
+    n,
+    cap,
+    tok_ref,
+    route_ref,
+    gate_ref,
+    up_hbm,
+    down_hbm,
+    grad_ref,
+    out_ref,
+    tgrad_ref,
+    pgrad_ref,
+    ugrad_ref,
+    dgrad_ref,
+    up,
+    down,
+    tok_send,
+    grad_send,
+    rows,
+    grads,
+    rows_t,
+    hidden,
+    slope,
+    dpre,
+    mine,
+    merge_send,
+    merge_recv,
+    ret_send,
+    ret_recv,
+    placing_t,
+    weight_sem,
+    ep_send,
+    ep_recv,
+    dp_send,
+    dp_recv,
+    merge_ssem,
+    merge_rsem,
+):
+    me, core = lax.axis_index("ep"), lax.axis_index("dp")
+    partner = (me, 1 - core)
+    slots = n * cap
+    count, width = tok_ref.shape
+    units = up.shape[1]
+
+    barrier = pltpu.get_barrier_semaphore()
+
+    @pl.loop(1, n)
+    def _(k):
+        pl.semaphore_signal(
+            barrier, inc=1, device_id=(lax.rem(me + k, n), core), device_id_type=MESH
+        )
+
+    pl.semaphore_signal(barrier, inc=1, device_id=partner, device_id_type=MESH)
+    up_copy = pltpu.make_async_copy(up_hbm.at[0], up, weight_sem.at[0])
+    down_copy = pltpu.make_async_copy(down_hbm.at[0], down, weight_sem.at[1])
+    up_copy.start()
+    down_copy.start()
+
+    def remote(src, dst, ssem, rsem, device):
+        return pltpu.make_async_remote_copy(
+            src_ref=src,
+            dst_ref=dst,
+            send_sem=ssem,
+            recv_sem=rsem,
+            device_id=device,
+            device_id_type=MESH,
+        )
+
+    def exchange(kind, src, dst, peer, slot):
+        return remote(
+            src.at[row_block(peer * cap, cap)],
+            dst.at[row_block(slot * cap, cap)],
+            ep_send.at[kind, peer],
+            ep_recv.at[kind, slot],
+            (peer, core),
+        )
+
+    def send_all(kind, src, dst):
+        @pl.loop(1, n)
+        def _(k):
+            exchange(kind, src, dst, lax.rem(me + k, n), me).start()
+
+        dst[row_block(me * cap, cap), :] = src[row_block(me * cap, cap), :]
+
+    def wait_block(kind, src, dst, source):
+        exchange(kind, src, dst, source, source).wait_recv()
+
+    def forward(kind, buf, source):
+        return remote(
+            buf.at[row_block(source * cap, cap)],
+            buf.at[row_block(slots + source * cap, cap)],
+            dp_send.at[kind, source],
+            dp_recv.at[kind, source],
+            partner,
+        )
+
+    def share(kind, src, dst):
+        forward(kind, dst, me).start()
+
+        @pl.loop(1, n)
+        def _(k):
+            source = lax.rem(me + k, n)
+            wait_block(kind, src, dst, source)
+            forward(kind, dst, source).start()
+
+        @pl.loop(0, n)
+        def _(k):
+            forward(kind, dst, k).wait_recv()
+
+    eye = lax.broadcasted_iota(jnp.int32, (count, count), 0) == lax.broadcasted_iota(
+        jnp.int32, (count, count), 1
+    )
+
+    def to_column(row):
+        return jnp.sum(jnp.where(eye, row, 0.0), axis=1, keepdims=True)
+
+    expert = route_ref[...]
+    onehot = (lax.broadcasted_iota(jnp.int32, (n, count), 0) == expert).astype(jnp.float32)
+    before = (
+        lax.broadcasted_iota(jnp.int32, (count, count), 0)
+        < lax.broadcasted_iota(jnp.int32, (count, count), 1)
+    ).astype(jnp.float32)
+    earlier = jnp.dot(
+        onehot.astype(jnp.bfloat16),
+        before.astype(jnp.bfloat16),
+        preferred_element_type=jnp.float32,
+    )
+    target = expert.astype(jnp.float32) * cap + jnp.sum(earlier * onehot, axis=0, keepdims=True)
+    slot_rows = lax.broadcasted_iota(jnp.int32, (slots, count), 0).astype(jnp.float32)
+    placing = (slot_rows == target).astype(jnp.float32).astype(jnp.bfloat16)
+    tok_send[...] = jnp.dot(
+        placing, tok_ref[...], preferred_element_type=jnp.float32
+    ).astype(jnp.bfloat16)
+    pl.semaphore_wait(barrier, n)
+    send_all(0, tok_send, rows)
+
+    gate = to_column(gate_ref[...])
+    scaled = (gate * grad_ref[...].astype(jnp.float32)).astype(jnp.bfloat16)
+    grad_send[...] = jnp.dot(
+        placing, scaled, preferred_element_type=jnp.float32
+    ).astype(jnp.bfloat16)
+    send_all(1, grad_send, grads)
+    slot_cols = lax.broadcasted_iota(jnp.int32, (count, slots), 1).astype(jnp.float32)
+    placing_t[...] = (slot_cols == to_column(target)).astype(jnp.float32).astype(jnp.bfloat16)
+
+    share(0, tok_send, rows)
+    up_copy.wait()
+
+    @pl.loop(0, units // CHUNK)
+    def _(c):
+        cols = pl.ds(pl.multiple_of(c * CHUNK, CHUNK), CHUNK)
+        pre = jnp.dot(rows[...], up[:, cols], preferred_element_type=jnp.float32)
+        square = pre * pre
+        bend = jnp.tanh(SCALE * pre * (1.0 + CUBIC * square))
+        half = 0.5 + 0.5 * bend
+        hidden[:, cols] = (pre * half).astype(jnp.bfloat16)
+        slope[:, cols] = half + (0.5 * SCALE) * pre * (1.0 - bend * bend) * (
+            1.0 + (3.0 * CUBIC) * square
+        )
+
+    down_copy.wait()
+
+    def merge(kind, product):
+        @pl.loop(0, width // CHUNK)
+        def _(c):
+            cols = pl.ds(pl.multiple_of(c * CHUNK, CHUNK), CHUNK)
+            merge_send[kind, :, cols] = product(slots, cols).astype(jnp.bfloat16)
+
+        swap = remote(
+            merge_send.at[kind],
+            merge_recv.at[kind],
+            merge_ssem.at[kind],
+            merge_rsem.at[kind],
+            partner,
+        )
+        swap.start()
+
+        @pl.loop(0, width // CHUNK)
+        def _(c):
+            cols = pl.ds(pl.multiple_of(c * CHUNK, CHUNK), CHUNK)
+            mine[:, cols] = product(0, cols)
+
+        swap.wait_recv()
+        ret_send[kind] = (mine[...] + merge_recv[kind].astype(jnp.float32)).astype(jnp.bfloat16)
+        send_all(2 + kind, ret_send.at[kind], ret_recv.at[kind])
+
+    def out_product(start, cols):
+        return jnp.dot(
+            hidden[start : start + slots, :], down[:, cols], preferred_element_type=jnp.float32
+        )
+
+    merge(0, out_product)
+
+    share(1, grad_send, grads)
+    across = (((1,), (1,)), ((), ()))
+
+    @pl.loop(0, units // CHUNK)
+    def _(c):
+        cols = pl.ds(pl.multiple_of(c * CHUNK, CHUNK), CHUNK)
+        dhid = lax.dot_general(
+            grads[...], down[cols, :], across, preferred_element_type=jnp.float32
+        )
+        dpre[:, cols] = (dhid * slope[:, cols]).astype(jnp.bfloat16)
+
+    def in_product(start, cols):
+        return lax.dot_general(
+            dpre[start : start + slots, :],
+            up[cols, :],
+            across,
+            preferred_element_type=jnp.float32,
+        )
+
+    merge(1, in_product)
+
+    rows_t[...] = rows[...].T
+
+    @pl.loop(0, units // CHUNK)
+    def _(c):
+        cols = pl.ds(pl.multiple_of(c * CHUNK, CHUNK), CHUNK)
+        ugrad_ref[0, :, cols] = jnp.dot(
+            rows_t[...], dpre[:, cols], preferred_element_type=jnp.float32
+        ).astype(jnp.bfloat16)
+        dgrad_ref[0, cols, :] = lax.dot_general(
+            hidden[:, cols],
+            grads[...],
+            (((0,), (0,)), ((), ())),
+            preferred_element_type=jnp.float32,
+        ).astype(jnp.bfloat16)
+
+    def collect(kind):
+        @pl.loop(1, n)
+        def _(k):
+            wait_block(2 + kind, ret_send.at[kind], ret_recv.at[kind], lax.rem(me + k, n))
+
+        return jnp.dot(placing_t[...], ret_recv[kind], preferred_element_type=jnp.float32)
+
+    returned = collect(0)
+    out_ref[...] = (to_column(gate_ref[...]) * returned).astype(jnp.bfloat16)
+    dots = jnp.sum(grad_ref[...].astype(jnp.float32) * returned, axis=1, keepdims=True)
+    pgrad_ref[...] = jnp.sum(jnp.where(eye, dots, 0.0), axis=0, keepdims=True)
+    tgrad_ref[...] = collect(1).astype(jnp.bfloat16)
+
+    @pl.loop(1, n)
+    def _(k):
+        peer = lax.rem(me + k, n)
+        exchange(0, tok_send, rows, peer, me).wait_send()
+        exchange(1, grad_send, grads, peer, me).wait_send()
+        exchange(2, ret_send.at[0], ret_recv.at[0], peer, me).wait_send()
+        exchange(3, ret_send.at[1], ret_recv.at[1], peer, me).wait_send()
+
+    @pl.loop(0, n)
+    def _(k):
+        forward(0, rows, k).wait_send()
+        forward(1, grads, k).wait_send()
+
+    for kind in range(2):
+        remote(
+            merge_send.at[kind],
+            merge_recv.at[kind],
+            merge_ssem.at[kind],
+            merge_rsem.at[kind],
+            partner,
+        ).wait_send()
+
+
+def local_fused(tokens, routing, gate_prob, up_weight, down_weight, out_grad):
+    n = lax.axis_size("ep")
+    count, width = tokens.shape
+    units = up_weight.shape[2]
+    cap = 2 * count // n
+    slots = n * cap
+    low, wide = jnp.bfloat16, jnp.float32
+    vmem = pl.BlockSpec(memory_space=pltpu.VMEM)
+    anywhere = pl.BlockSpec(memory_space=pl.ANY)
+    dma = pltpu.SemaphoreType.DMA
+    output, token_grad, prob_grad, up_grad, down_grad = pl.pallas_call(
+        functools.partial(kernel, n, cap),
+        out_shape=(
+            jax.ShapeDtypeStruct((count, width), low),
+            jax.ShapeDtypeStruct((count, width), low),
+            jax.ShapeDtypeStruct((1, count), wide),
+            jax.ShapeDtypeStruct(up_weight.shape, low),
+            jax.ShapeDtypeStruct(down_weight.shape, low),
+        ),
+        in_specs=[vmem, vmem, vmem, anywhere, anywhere, vmem],
+        out_specs=(vmem,) * 5,
+        scratch_shapes=[
+            pltpu.VMEM((width, units), low),
+            pltpu.VMEM((units, width), low),
+            pltpu.VMEM((slots, width), low),
+            pltpu.VMEM((slots, width), low),
+            pltpu.VMEM((2 * slots, width), low),
+            pltpu.VMEM((2 * slots, width), low),
+            pltpu.VMEM((width, 2 * slots), low),
+            pltpu.VMEM((2 * slots, units), low),
+            pltpu.VMEM((2 * slots, units), wide),
+            pltpu.VMEM((2 * slots, units), low),
+            pltpu.VMEM((slots, width), wide),
+            pltpu.VMEM((2, slots, width), low),
+            pltpu.VMEM((2, slots, width), low),
+            pltpu.VMEM((2, slots, width), low),
+            pltpu.VMEM((2, slots, width), low),
+            pltpu.VMEM((count, slots), low),
+            dma((2,)),
+            dma((4, n)),
+            dma((4, n)),
+            dma((2, n)),
+            dma((2, n)),
+            dma((2,)),
+            dma((2,)),
+        ],
+        compiler_params=pltpu.CompilerParams(
+            collective_id=0, has_side_effects=True, vmem_limit_bytes=44 << 20
+        ),
+        cost_estimate=pl.CostEstimate(
+            flops=12 * 2 * slots * width * units,
+            bytes_accessed=8 * width * units,
+            transcendentals=2 * slots * units,
+        ),
+    )(
+        tokens,
+        routing.reshape(1, count),
+        gate_prob.reshape(1, count),
+        up_weight,
+        down_weight,
+        out_grad,
+    )
+    return (output, token_grad, prob_grad.reshape(count), up_grad, down_grad)
+
+
+def local(tokens, routing, gate_prob, up_weight, down_weight, out_grad):
+    n = lax.axis_size("ep")
+    count, width = tokens.shape
+    fits = (
+        up_weight.shape[0] == 1
+        and lax.axis_size("dp") == 2
+        and (2 * count // n) % TILE == 0
+        and (2 * count) % n == 0
+        and up_weight.shape[2] % CHUNK == 0
+        and width % CHUNK == 0
+    )
+    run = local_fused if fits else local_plain
+    return run(tokens, routing, gate_prob, up_weight, down_weight, out_grad)
+
+
 def solution(mesh):
     placed = (
         P(("ep", "dp"), None),

time: 125 us -> 58.1 us (0.46)
  the two profiles are of different devices: /device:TPU:0 before, /device:TPU:28 now
where the time goes in v1:
time: 58.1 us; the launch traced here: 57.9 us
  Pallas kernels  46 us (79%)
  local copies, waits for them, and re-layouts  11.2 us (19%)
  between operations  0.66 us (1%)
    pallas_call x1, Pallas kernels, local_fused(): pl.pallas_call(functools.partial(kernel, n, cap), out_shape=(jax.ShapeDty...  46 us
    unnamed x17, local copies, waits for them, and re-layouts  11.2 us

profile of v1, /device:TPU:28, one launch (start us, length us, event | category | flops | bytes accessed | tf_op | source)
XLA Modules:
  0.0 57.9 jit_solution(16100627061431193249)
XLA Ops:
  0.6 0.0 copy-start
  0.6 1.7 %copy-done = bf16[1,768,1536]{2,1,0:T(8,128)(2,1)S(1)} copy-done((bf16[1,768,1536]{2,1,0:T(8,128)(2,1)S(1)}, bf16[1,768,1536]{2,1,0:T(8,128)(2,1)}, u32[]{:S(2)}) %copy-start) | copy-done | bytes 2359320
  2.3 0.0 copy-start.1
  2.3 1.7 %copy-done.1 = bf16[1,1536,768]{2,1,0:T(8,128)(2,1)S(1)} copy-done((bf16[1,1536,768]{2,1,0:T(8,128)(2,1)S(1)}, bf16[1,1536,768]{2,1,0:T(8,128)(2,1)}, u32[]{:S(2)}) %copy-start.1) | copy-done | bytes 2359320
  4.0 0.0 copy-start.2
  4.0 0.9 %copy-done.2 = bf16[128,768]{1,0:T(8,128)(2,1)S(1)} copy-done((bf16[128,768]{1,0:T(8,128)(2,1)S(1)}, bf16[128,768]{1,0:T(8,128)(2,1)}, u32[]{:S(2)}) %copy-start.2) | copy-done | bytes 196632
  4.9 0.0 copy-start.3
  4.9 0.9 %copy-done.3 = bf16[128,768]{1,0:T(8,128)(2,1)S(1)} copy-done((bf16[128,768]{1,0:T(8,128)(2,1)S(1)}, bf16[128,768]{1,0:T(8,128)(2,1)}, u32[]{:S(2)}) %copy-start.3) | copy-done | bytes 196632
  5.8 0.0 copy-start.4
  5.8 0.7 %copy-done.4 = s32[128,1]{0,1:T(1,128)S(1)} copy-done((s32[128,1]{0,1:T(1,128)S(1)}, s32[128,1]{0,1:T(1,128)}, u32[]{:S(2)}) %copy-start.4) | copy-done | bytes 536
  6.5 0.0 copy-start.5
  6.5 0.7 %copy-done.5 = f32[128]{0:T(128)S(1)} copy-done((f32[128]{0:T(128)S(1)}, f32[128]{0:T(128)}, u32[]{:S(2)}) %copy-start.5) | copy-done | bytes 536
  7.1 46.0 %shard_map.101 = (bf16[128,768]{1,0:T(8,128)(2,1)S(1)}, bf16[128,768]{1,0:T(8,128)(2,1)S(1)}, f32[1,128]{1,0:T(1,128)S(1)}, bf16[1,768,1536]{2,1,0:T(8,128)(2,1)S(1)}, bf16[1,1536,768]{2,1,0:T(8,128)(2,1)S(1)}) custom-call(bf16[128,768]{1,0:T(8,128)(2,1)S(1)} %copy-done.2, s32[1,128]{1,0:T(1,128)S(1)} %bitcast.3, f32[1,128]{1,0:T(1,128)S(1)} %bitcast.4, ...), custom_call_target="tpu_custom_call" | custom-call | flops 7247757312 | bytes 9437184 | tf_op jit(solution)/shard_map/pallas_call | solution.py:359
  53.2 0.7 %copy.16 = bf16[128,768]{1,0:T(8,128)(2,1)} copy(bf16[128,768]{1,0:T(8,128)(2,1)S(1)} %get-tuple-element.20) | data formatting | bytes 393216
  53.9 0.7 %copy.17 = bf16[128,768]{1,0:T(8,128)(2,1)} copy(bf16[128,768]{1,0:T(8,128)(2,1)S(1)} %get-tuple-element.21) | data formatting | bytes 393216
  54.5 0.5 copy.18
  55.1 1.4 %copy.19 = bf16[1,768,1536]{2,1,0:T(8,128)(2,1)} copy(bf16[1,768,1536]{2,1,0:T(8,128)(2,1)S(1)} %get-tuple-element.23) | data formatting | bytes 4718592
  56.5 1.4 %copy.20 = bf16[1,1536,768]{2,1,0:T(8,128)(2,1)} copy(bf16[1,1536,768]{2,1,0:T(8,128)(2,1)S(1)} %get-tuple-element.24) | data formatting | bytes 4718592
Async XLA Ops:
  0.6 1.7 %copy-start = (bf16[1,768,1536]{2,1,0:T(8,128)(2,1)S(1)}, bf16[1,768,1536]{2,1,0:T(8,128)(2,1)}, u32[]{:S(2)}) copy-start(bf16[1,768,1536]{2,1,0:T(8,128)(2,1)} %up_hbm.1) | copy-start | bytes 7077892
  2.3 1.7 %copy-start.1 = (bf16[1,1536,768]{2,1,0:T(8,128)(2,1)S(1)}, bf16[1,1536,768]{2,1,0:T(8,128)(2,1)}, u32[]{:S(2)}) copy-start(bf16[1,1536,768]{2,1,0:T(8,128)(2,1)} %down_hbm.1) | copy-start | bytes 7077892
  4.0 0.9 %copy-start.2 = (bf16[128,768]{1,0:T(8,128)(2,1)S(1)}, bf16[128,768]{1,0:T(8,128)(2,1)}, u32[]{:S(2)}) copy-start(bf16[128,768]{1,0:T(8,128)(2,1)} %tok_ref.1) | copy-start | bytes 589828
  4.9 0.9 %copy-start.3 = (bf16[128,768]{1,0:T(8,128)(2,1)S(1)}, bf16[128,768]{1,0:T(8,128)(2,1)}, u32[]{:S(2)}) copy-start(bf16[128,768]{1,0:T(8,128)(2,1)} %grad_ref.1) | copy-start | bytes 589828
  5.8 0.7 %copy-start.4 = (s32[128,1]{0,1:T(1,128)S(1)}, s32[128,1]{0,1:T(1,128)}, u32[]{:S(2)}) copy-start(s32[128,1]{0,1:T(1,128)} %param.7) | copy-start | bytes 1540
  6.5 0.7 %copy-start.5 = (f32[128]{0:T(128)S(1)}, f32[128]{0:T(128)}, u32[]{:S(2)}) copy-start(f32[128]{0:T(128)} %param.8) | copy-start | bytes 1540

commit v2 on v1

--- a/solution.py
+++ b/solution.py
@@ -84,17 +84,23 @@
 def kernel(
     n,
     cap,
+    tok_hbm,
+    route_hbm,
+    gate_hbm,
+    up_hbm,
+    down_hbm,
+    grad_hbm,
+    out_ref,
+    tgrad_ref,
+    pgrad_ref,
+    ugrad_hbm,
+    dgrad_hbm,
+    ugrad_ref,
+    dgrad_ref,
     tok_ref,
     route_ref,
     gate_ref,
-    up_hbm,
-    down_hbm,
     grad_ref,
-    out_ref,
-    tgrad_ref,
-    pgrad_ref,
-    ugrad_ref,
-    dgrad_ref,
     up,
     down,
     tok_send,
@@ -125,6 +131,19 @@
     count, width = tok_ref.shape
     units = up.shape[1]
 
+    staged = [
+        pltpu.make_async_copy(far, near, weight_sem.at[2 + i])
+        for i, (far, near) in enumerate(
+            (
+                (route_hbm, route_ref),
+                (tok_hbm, tok_ref),
+                (gate_hbm, gate_ref),
+                (grad_hbm, grad_ref),
+            )
+        )
+    ]
+    for copy in staged:
+        copy.start()
     barrier = pltpu.get_barrier_semaphore()
 
     @pl.loop(1, n)
@@ -186,6 +205,7 @@
             wait_block(kind, src, dst, source)
             forward(kind, dst, source).start()
 
+    def shared(kind, dst):
         @pl.loop(0, n)
         def _(k):
             forward(kind, dst, k).wait_recv()
@@ -197,6 +217,7 @@
     def to_column(row):
         return jnp.sum(jnp.where(eye, row, 0.0), axis=1, keepdims=True)
 
+    staged[0].wait()
     expert = route_ref[...]
     onehot = (lax.broadcasted_iota(jnp.int32, (n, count), 0) == expert).astype(jnp.float32)
     before = (
@@ -211,12 +232,15 @@
     target = expert.astype(jnp.float32) * cap + jnp.sum(earlier * onehot, axis=0, keepdims=True)
     slot_rows = lax.broadcasted_iota(jnp.int32, (slots, count), 0).astype(jnp.float32)
     placing = (slot_rows == target).astype(jnp.float32).astype(jnp.bfloat16)
+    staged[1].wait()
     tok_send[...] = jnp.dot(
         placing, tok_ref[...], preferred_element_type=jnp.float32
     ).astype(jnp.bfloat16)
     pl.semaphore_wait(barrier, n)
     send_all(0, tok_send, rows)
 
+    staged[2].wait()
+    staged[3].wait()
     gate = to_column(gate_ref[...])
     scaled = (gate * grad_ref[...].astype(jnp.float32)).astype(jnp.bfloat16)
     grad_send[...] = jnp.dot(
@@ -227,6 +251,7 @@
     placing_t[...] = (slot_cols == to_column(target)).astype(jnp.float32).astype(jnp.bfloat16)
 
     share(0, tok_send, rows)
+    shared(0, rows)
     up_copy.wait()
 
     @pl.loop(0, units // CHUNK)
@@ -243,7 +268,7 @@
 
     down_copy.wait()
 
-    def merge(kind, product):
+    def merge(kind, product, meanwhile):
         @pl.loop(0, width // CHUNK)
         def _(c):
             cols = pl.ds(pl.multiple_of(c * CHUNK, CHUNK), CHUNK)
@@ -263,6 +288,7 @@
             cols = pl.ds(pl.multiple_of(c * CHUNK, CHUNK), CHUNK)
             mine[:, cols] = product(0, cols)
 
+        meanwhile()
         swap.wait_recv()
         ret_send[kind] = (mine[...] + merge_recv[kind].astype(jnp.float32)).astype(jnp.bfloat16)
         send_all(2 + kind, ret_send.at[kind], ret_recv.at[kind])
@@ -272,9 +298,9 @@
             hidden[start : start + slots, :], down[:, cols], preferred_element_type=jnp.float32
         )
 
-    merge(0, out_product)
-
-    share(1, grad_send, grads)
+    merge(0, out_product, lambda: share(1, grad_send, grads))
+
+    shared(1, grads)
     across = (((1,), (1,)), ((), ()))
 
     @pl.loop(0, units // CHUNK)
@@ -293,22 +319,29 @@
             preferred_element_type=jnp.float32,
         )
 
-    merge(1, in_product)
+    merge(1, in_product, lambda: None)
 
     rows_t[...] = rows[...].T
 
     @pl.loop(0, units // CHUNK)
     def _(c):
         cols = pl.ds(pl.multiple_of(c * CHUNK, CHUNK), CHUNK)
-        ugrad_ref[0, :, cols] = jnp.dot(
+        ugrad_ref[:, cols] = jnp.dot(
             rows_t[...], dpre[:, cols], preferred_element_type=jnp.float32
         ).astype(jnp.bfloat16)
-        dgrad_ref[0, cols, :] = lax.dot_general(
+        dgrad_ref[cols, :] = lax.dot_general(
             hidden[:, cols],
             grads[...],
             (((0,), (0,)), ((), ())),
             preferred_element_type=jnp.float32,
         ).astype(jnp.bfloat16)
+
+    writes = (
+        pltpu.make_async_copy(ugrad_ref, ugrad_hbm.at[0], weight_sem.at[6]),
+        pltpu.make_async_copy(dgrad_ref, dgrad_hbm.at[0], weight_sem.at[7]),
+    )
+    for write in writes:
+        write.start()
 
     def collect(kind):
         @pl.loop(1, n)
@@ -336,6 +369,8 @@
         forward(0, rows, k).wait_send()
         forward(1, grads, k).wait_send()
 
+    for write in writes:
+        write.wait()
     for kind in range(2):
         remote(
             merge_send.at[kind],
@@ -354,7 +389,7 @@
     slots = n * cap
     low, wide = jnp.bfloat16, jnp.float32
     vmem = pl.BlockSpec(memory_space=pltpu.VMEM)
-    anywhere = pl.BlockSpec(memory_space=pl.ANY)
+    far = pl.BlockSpec(memory_space=pltpu.HBM)
     dma = pltpu.SemaphoreType.DMA
     output, token_grad, prob_grad, up_grad, down_grad = pl.pallas_call(
         functools.partial(kernel, n, cap),
@@ -365,9 +400,15 @@
             jax.ShapeDtypeStruct(up_weight.shape, low),
             jax.ShapeDtypeStruct(down_weight.shape, low),
         ),
-        in_specs=[vmem, vmem, vmem, anywhere, anywhere, vmem],
-        out_specs=(vmem,) * 5,
+        in_specs=[far] * 6,
+        out_specs=(vmem, vmem, vmem, far, far),
         scratch_shapes=[
+            pltpu.VMEM((width, units), low),
+            pltpu.VMEM((units, width), low),
+            pltpu.VMEM((count, width), low),
+            pltpu.VMEM((1, count), jnp.int32),
+            pltpu.VMEM((1, count), wide),
+            pltpu.VMEM((count, width), low),
             pltpu.VMEM((width, units), low),
             pltpu.VMEM((units, width), low),
             pltpu.VMEM((slots, width), low),
@@ -384,7 +425,7 @@
             pltpu.VMEM((2, slots, width), low),
             pltpu.VMEM((2, slots, width), low),
             pltpu.VMEM((count, slots), low),
-            dma((2,)),
+            dma((8,)),
             dma((4, n)),
             dma((4, n)),
             dma((2, n)),
@@ -393,7 +434,7 @@
             dma((2,)),
         ],
         compiler_params=pltpu.CompilerParams(
-            collective_id=0, has_side_effects=True, vmem_limit_bytes=44 << 20
+            collective_id=0, has_side_effects=True, vmem_limit_bytes=58 << 20
         ),
         cost_estimate=pl.CostEstimate(
             flops=12 * 2 * slots * width * units,

time: 58.1 us -> 57.4 us (0.988)
  local copies, waits for them, and re-layouts: 11.2 us -> 9.18 us
  Pallas kernels: 46 us -> 47.4 us
    unnamed x17 -> x7, local copies, waits for them, and re-layouts: 11.2 us -> 9.18 us
    pallas_call x1, Pallas kernels: 46 us -> 47.4 us  [local_fused(): pl.pallas_call(functools.partial(kernel, n, cap), out_shape=(jax.ShapeDty...]
where the time goes in v2:
time: 57.4 us; the launch traced here: 57.3 us
  Pallas kernels  47.4 us (83%)
  local copies, waits for them, and re-layouts  9.18 us (16%)
  between operations  0.64 us (1%)
    pallas_call x1, Pallas kernels, local_fused(): pl.pallas_call(functools.partial(kernel, n, cap), out_shape=(jax.ShapeDty...  47.4 us
    unnamed x7, local copies, waits for them, and re-layouts  9.18 us

profile of v2, /device:TPU:28, one launch (start us, length us, event | category | flops | bytes accessed | tf_op | source)
XLA Modules:
  0.0 57.3 jit_solution(3485277584971168234)
XLA Ops:
  0.6 47.4 %shard_map.101 = (bf16[128,768]{1,0:T(8,128)(2,1)}, bf16[128,768]{1,0:T(8,128)(2,1)}, f32[1,128]{1,0:T(1,128)}, bf16[1,768,1536]{2,1,0:T(8,128)(2,1)}, bf16[1,1536,768]{2,1,0:T(8,128)(2,1)}) custom-call(bf16[128,768]{1,0:T(8,128)(2,1)} %tok_hbm.1, s32[1,128]{1,0:T(1,128)} %bitcast.3, f32[1,128]{1,0:T(1,128)} %bitcast.4, bf16[1,768,1536]{2,1,0:T(8,128)(2,1)} %up_hbm.1, ...), custom_call_target="tpu_custom_call" | custom-call | flops 7247757312 | bytes 9437184 | tf_op jit(solution)/shard_map/pallas_call | solution.py:394
  48.1 1.6 %copy.16 = bf16[128,768]{1,0:T(8,128)(2,1)} copy(bf16[128,768]{1,0:T(8,128)(2,1)} %get-tuple-element.20) | data formatting | bytes 393216
  49.7 1.6 %copy.17 = bf16[128,768]{1,0:T(8,128)(2,1)} copy(bf16[128,768]{1,0:T(8,128)(2,1)} %get-tuple-element.21) | data formatting | bytes 393216
  51.3 1.2 %copy.18 = f32[128]{0:T(128)} copy(f32[128]{0:T(128)} %bitcast.5) | data formatting | bytes 1024
  52.5 0.0 copy-start
  52.5 3.4 %copy.19 = bf16[1,768,1536]{2,1,0:T(8,128)(2,1)} copy(bf16[1,768,1536]{2,1,0:T(8,128)(2,1)} %get-tuple-element.23) | data formatting | bytes 4718592
  55.8 0.0 copy-done
  55.9 1.4 %copy.20 = bf16[1,1536,768]{2,1,0:T(8,128)(2,1)} copy(bf16[1,1536,768]{2,1,0:T(8,128)(2,1)S(1)} %copy-done) | data formatting | bytes 4718592
Async XLA Ops:
  52.5 3.4 %copy-start = (bf16[1,1536,768]{2,1,0:T(8,128)(2,1)S(1)}, bf16[1,1536,768]{2,1,0:T(8,128)(2,1)}, u32[]{:S(2)}) copy-start(bf16[1,1536,768]{2,1,0:T(8,128)(2,1)} %get-tuple-element.24) | copy-start | bytes 7077892

commit v3 on v2

--- a/solution.py
+++ b/solution.py
@@ -93,8 +93,6 @@
     out_ref,
     tgrad_ref,
     pgrad_ref,
-    ugrad_hbm,
-    dgrad_hbm,
     ugrad_ref,
     dgrad_ref,
     tok_ref,
@@ -196,7 +194,7 @@
             partner,
         )
 
-    def share(kind, src, dst):
+    def share(kind, src, dst, then):
         forward(kind, dst, me).start()
 
         @pl.loop(1, n)
@@ -204,6 +202,7 @@
             source = lax.rem(me + k, n)
             wait_block(kind, src, dst, source)
             forward(kind, dst, source).start()
+            then(k)
 
     def shared(kind, dst):
         @pl.loop(0, n)
@@ -246,11 +245,14 @@
     grad_send[...] = jnp.dot(
         placing, scaled, preferred_element_type=jnp.float32
     ).astype(jnp.bfloat16)
-    send_all(1, grad_send, grads)
+    grads[row_block(me * cap, cap), :] = grad_send[row_block(me * cap, cap), :]
     slot_cols = lax.broadcasted_iota(jnp.int32, (count, slots), 1).astype(jnp.float32)
     placing_t[...] = (slot_cols == to_column(target)).astype(jnp.float32).astype(jnp.bfloat16)
 
-    share(0, tok_send, rows)
+    def send_grads(k):
+        exchange(1, grad_send, grads, lax.rem(me + k, n), me).start()
+
+    share(0, tok_send, rows, send_grads)
     shared(0, rows)
     up_copy.wait()
 
@@ -298,7 +300,7 @@
             hidden[start : start + slots, :], down[:, cols], preferred_element_type=jnp.float32
         )
 
-    merge(0, out_product, lambda: share(1, grad_send, grads))
+    merge(0, out_product, lambda: share(1, grad_send, grads, lambda k: None))
 
     shared(1, grads)
     across = (((1,), (1,)), ((), ()))
@@ -326,22 +328,15 @@
     @pl.loop(0, units // CHUNK)
     def _(c):
         cols = pl.ds(pl.multiple_of(c * CHUNK, CHUNK), CHUNK)
-        ugrad_ref[:, cols] = jnp.dot(
+        ugrad_ref[0, :, cols] = jnp.dot(
             rows_t[...], dpre[:, cols], preferred_element_type=jnp.float32
         ).astype(jnp.bfloat16)
-        dgrad_ref[cols, :] = lax.dot_general(
+        dgrad_ref[0, cols, :] = lax.dot_general(
             hidden[:, cols],
             grads[...],
             (((0,), (0,)), ((), ())),
             preferred_element_type=jnp.float32,
         ).astype(jnp.bfloat16)
-
-    writes = (
-        pltpu.make_async_copy(ugrad_ref, ugrad_hbm.at[0], weight_sem.at[6]),
-        pltpu.make_async_copy(dgrad_ref, dgrad_hbm.at[0], weight_sem.at[7]),
-    )
-    for write in writes:
-        write.start()
 
     def collect(kind):
         @pl.loop(1, n)
@@ -369,8 +364,6 @@
         forward(0, rows, k).wait_send()
         forward(1, grads, k).wait_send()
 
-    for write in writes:
-        write.wait()
     for kind in range(2):
         remote(
             merge_send.at[kind],
@@ -401,10 +394,8 @@
             jax.ShapeDtypeStruct(down_weight.shape, low),
         ),
         in_specs=[far] * 6,
-        out_specs=(vmem, vmem, vmem, far, far),
+        out_specs=(vmem,) * 5,
         scratch_shapes=[
-            pltpu.VMEM((width, units), low),
-            pltpu.VMEM((units, width), low),
             pltpu.VMEM((count, width), low),
             pltpu.VMEM((1, count), jnp.int32),
             pltpu.VMEM((1, count), wide),
@@ -425,7 +416,7 @@
             pltpu.VMEM((2, slots, width), low),
             pltpu.VMEM((2, slots, width), low),
             pltpu.VMEM((count, slots), low),
-            dma((8,)),
+            dma((6,)),
             dma((4, n)),
             dma((4, n)),
             dma((2, n)),
@@ -434,7 +425,7 @@
             dma((2,)),
         ],
         compiler_params=pltpu.CompilerParams(
-            collective_id=0, has_side_effects=True, vmem_limit_bytes=58 << 20
+            collective_id=0, has_side_effects=True, vmem_limit_bytes=48 << 20
         ),
         cost_estimate=pl.CostEstimate(
             flops=12 * 2 * slots * width * units,

time: 57.4 us -> 54.1 us (0.943)
  Pallas kernels: 47.4 us -> 45.2 us
  local copies, waits for them, and re-layouts: 9.18 us -> 7.83 us
    pallas_call x1, Pallas kernels: 47.4 us -> 45.2 us  [local_fused(): pl.pallas_call(functools.partial(kernel, n, cap), out_shape=(jax.ShapeDty...]
    unnamed x7 -> x13, local copies, waits for them, and re-layouts: 9.18 us -> 7.83 us
where the time goes in v3:
time: 54.1 us; the launch traced here: 53.7 us
  Pallas kernels  45.2 us (84%)
  local copies, waits for them, and re-layouts  7.83 us (14%)
  between operations  0.65 us (1%)
    pallas_call x1, Pallas kernels, local_fused(): pl.pallas_call(functools.partial(kernel, n, cap), out_shape=(jax.ShapeDty...  45.2 us
    unnamed x13, local copies, waits for them, and re-layouts  7.83 us

profile of v3, /device:TPU:28, one launch (start us, length us, event | category | flops | bytes accessed | tf_op | source)
XLA Modules:
  0.0 53.7 jit_solution(16304584164064918791)
XLA Ops:
  0.6 0.0 copy-start
  0.6 0.9 %copy-done = bf16[128,768]{1,0:T(8,128)(2,1)S(1)} copy-done((bf16[128,768]{1,0:T(8,128)(2,1)S(1)}, bf16[128,768]{1,0:T(8,128)(2,1)}, u32[]{:S(2)}) %copy-start) | copy-done | bytes 196632
  1.6 0.0 copy-start.1
  1.6 0.9 %copy-done.1 = bf16[128,768]{1,0:T(8,128)(2,1)S(1)} copy-done((bf16[128,768]{1,0:T(8,128)(2,1)S(1)}, bf16[128,768]{1,0:T(8,128)(2,1)}, u32[]{:S(2)}) %copy-start.1) | copy-done | bytes 196632
  2.5 0.0 copy-start.2
  2.5 0.7 %copy-done.2 = s32[128,1]{0,1:T(1,128)S(1)} copy-done((s32[128,1]{0,1:T(1,128)S(1)}, s32[128,1]{0,1:T(1,128)}, u32[]{:S(2)}) %copy-start.2) | copy-done | bytes 536
  3.1 0.0 copy-start.3
  3.1 0.7 %copy-done.3 = f32[128]{0:T(128)S(1)} copy-done((f32[128]{0:T(128)S(1)}, f32[128]{0:T(128)}, u32[]{:S(2)}) %copy-start.3) | copy-done | bytes 536
  3.8 45.2 %shard_map.101 = (bf16[128,768]{1,0:T(8,128)(2,1)S(1)}, bf16[128,768]{1,0:T(8,128)(2,1)S(1)}, f32[1,128]{1,0:T(1,128)S(1)}, bf16[1,768,1536]{2,1,0:T(8,128)(2,1)S(1)}, bf16[1,1536,768]{2,1,0:T(8,128)(2,1)S(1)}) custom-call(bf16[128,768]{1,0:T(8,128)(2,1)S(1)} %copy-done, s32[1,128]{1,0:T(1,128)S(1)} %bitcast.3, f32[1,128]{1,0:T(1,128)S(1)} %bitcast.4, ...), custom_call_target="tpu_custom_call" | custom-call | flops 7247757312 | bytes 9437184 | tf_op jit(solution)/shard_map/pallas_call | solution.py:387
  49.0 0.7 %copy.16 = bf16[128,768]{1,0:T(8,128)(2,1)} copy(bf16[128,768]{1,0:T(8,128)(2,1)S(1)} %get-tuple-element.20) | data formatting | bytes 393216
  49.7 0.7 %copy.17 = bf16[128,768]{1,0:T(8,128)(2,1)} copy(bf16[128,768]{1,0:T(8,128)(2,1)S(1)} %get-tuple-element.21) | data formatting | bytes 393216
  50.4 0.5 copy.18
  50.9 1.4 %copy.19 = bf16[1,768,1536]{2,1,0:T(8,128)(2,1)} copy(bf16[1,768,1536]{2,1,0:T(8,128)(2,1)S(1)} %get-tuple-element.23) | data formatting | bytes 4718592
  52.3 1.4 %copy.20 = bf16[1,1536,768]{2,1,0:T(8,128)(2,1)} copy(bf16[1,1536,768]{2,1,0:T(8,128)(2,1)S(1)} %get-tuple-element.24) | data formatting | bytes 4718592
Async XLA Ops:
  0.6 0.9 %copy-start = (bf16[128,768]{1,0:T(8,128)(2,1)S(1)}, bf16[128,768]{1,0:T(8,128)(2,1)}, u32[]{:S(2)}) copy-start(bf16[128,768]{1,0:T(8,128)(2,1)} %tok_hbm.1) | copy-start | bytes 589828
  1.6 0.9 %copy-start.1 = (bf16[128,768]{1,0:T(8,128)(2,1)S(1)}, bf16[128,768]{1,0:T(8,128)(2,1)}, u32[]{:S(2)}) copy-start(bf16[128,768]{1,0:T(8,128)(2,1)} %grad_hbm.1) | copy-start | bytes 589828
  2.5 0.7 %copy-start.2 = (s32[128,1]{0,1:T(1,128)S(1)}, s32[128,1]{0,1:T(1,128)}, u32[]{:S(2)}) copy-start(s32[128,1]{0,1:T(1,128)} %param.7) | copy-start | bytes 1540
  3.1 0.7 %copy-start.3 = (f32[128]{0:T(128)S(1)}, f32[128]{0:T(128)}, u32[]{:S(2)}) copy-start(f32[128]{0:T(128)} %param.8) | copy-start | bytes 1540

commit v4 on v3

--- a/solution.py
+++ b/solution.py
@@ -175,10 +175,13 @@
             (peer, core),
         )
 
+    def far_first(k):
+        return 1 + lax.rem(k + n // 2 - 2, n - 1)
+
     def send_all(kind, src, dst):
         @pl.loop(1, n)
         def _(k):
-            exchange(kind, src, dst, lax.rem(me + k, n), me).start()
+            exchange(kind, src, dst, lax.rem(me + far_first(k), n), me).start()
 
         dst[row_block(me * cap, cap), :] = src[row_block(me * cap, cap), :]
 
@@ -199,7 +202,7 @@
 
         @pl.loop(1, n)
         def _(k):
-            source = lax.rem(me + k, n)
+            source = lax.rem(me + n - far_first(k), n)
             wait_block(kind, src, dst, source)
             forward(kind, dst, source).start()
             then(k)
@@ -250,7 +253,7 @@
     placing_t[...] = (slot_cols == to_column(target)).astype(jnp.float32).astype(jnp.bfloat16)
 
     def send_grads(k):
-        exchange(1, grad_send, grads, lax.rem(me + k, n), me).start()
+        exchange(1, grad_send, grads, lax.rem(me + far_first(k), n), me).start()
 
     share(0, tok_send, rows, send_grads)
     shared(0, rows)

time: 54.1 us -> 60 us (1.11)
  the two profiles are of different devices: /device:TPU:28 before, /device:TPU:0 now
where the time goes in v4:
time: 60 us; the launch traced here: 59.8 us
  Pallas kernels  51.3 us (86%)
  local copies, waits for them, and re-layouts  7.83 us (13%)
  between operations  0.65 us (1%)
    pallas_call x1, Pallas kernels, local_fused(): pl.pallas_call(functools.partial(kernel, n, cap), out_shape=(jax.ShapeDty...  51.3 us
    unnamed x13, local copies, waits for them, and re-layouts  7.83 us

profile of v4, /device:TPU:0, one launch (start us, length us, event | category | flops | bytes accessed | tf_op | source)
XLA Modules:
  0.0 59.8 jit_solution(11436333591937312667)
XLA Ops:
  0.6 0.0 copy-start
  0.6 0.9 %copy-done = bf16[128,768]{1,0:T(8,128)(2,1)S(1)} copy-done((bf16[128,768]{1,0:T(8,128)(2,1)S(1)}, bf16[128,768]{1,0:T(8,128)(2,1)}, u32[]{:S(2)}) %copy-start) | copy-done | bytes 196632
  1.6 0.0 copy-start.1
  1.6 0.9 %copy-done.1 = bf16[128,768]{1,0:T(8,128)(2,1)S(1)} copy-done((bf16[128,768]{1,0:T(8,128)(2,1)S(1)}, bf16[128,768]{1,0:T(8,128)(2,1)}, u32[]{:S(2)}) %copy-start.1) | copy-done | bytes 196632
  2.5 0.0 copy-start.2
  2.5 0.7 %copy-done.2 = s32[128,1]{0,1:T(1,128)S(1)} copy-done((s32[128,1]{0,1:T(1,128)S(1)}, s32[128,1]{0,1:T(1,128)}, u32[]{:S(2)}) %copy-start.2) | copy-done | bytes 536
  3.1 0.0 copy-start.3
  3.1 0.7 %copy-done.3 = f32[128]{0:T(128)S(1)} copy-done((f32[128]{0:T(128)S(1)}, f32[128]{0:T(128)}, u32[]{:S(2)}) %copy-start.3) | copy-done | bytes 536
  3.8 51.3 %shard_map.101 = (bf16[128,768]{1,0:T(8,128)(2,1)S(1)}, bf16[128,768]{1,0:T(8,128)(2,1)S(1)}, f32[1,128]{1,0:T(1,128)S(1)}, bf16[1,768,1536]{2,1,0:T(8,128)(2,1)S(1)}, bf16[1,1536,768]{2,1,0:T(8,128)(2,1)S(1)}) custom-call(bf16[128,768]{1,0:T(8,128)(2,1)S(1)} %copy-done, s32[1,128]{1,0:T(1,128)S(1)} %bitcast.3, f32[1,128]{1,0:T(1,128)S(1)} %bitcast.4, ...), custom_call_target="tpu_custom_call" | custom-call | flops 7247757312 | bytes 9437184 | tf_op jit(solution)/shard_map/pallas_call | solution.py:390
  55.2 0.7 %copy.16 = bf16[128,768]{1,0:T(8,128)(2,1)} copy(bf16[128,768]{1,0:T(8,128)(2,1)S(1)} %get-tuple-element.20) | data formatting | bytes 393216
  55.8 0.7 %copy.17 = bf16[128,768]{1,0:T(8,128)(2,1)} copy(bf16[128,768]{1,0:T(8,128)(2,1)S(1)} %get-tuple-element.21) | data formatting | bytes 393216
  56.5 0.5 copy.18
  57.0 1.4 %copy.19 = bf16[1,768,1536]{2,1,0:T(8,128)(2,1)} copy(bf16[1,768,1536]{2,1,0:T(8,128)(2,1)S(1)} %get-tuple-element.23) | data formatting | bytes 4718592
  58.4 1.4 %copy.20 = bf16[1,1536,768]{2,1,0:T(8,128)(2,1)} copy(bf16[1,1536,768]{2,1,0:T(8,128)(2,1)S(1)} %get-tuple-element.24) | data formatting | bytes 4718592
Async XLA Ops:
  0.6 0.9 %copy-start = (bf16[128,768]{1,0:T(8,128)(2,1)S(1)}, bf16[128,768]{1,0:T(8,128)(2,1)}, u32[]{:S(2)}) copy-start(bf16[128,768]{1,0:T(8,128)(2,1)} %tok_hbm.1) | copy-start | bytes 589828
  1.6 0.9 %copy-start.1 = (bf16[128,768]{1,0:T(8,128)(2,1)S(1)}, bf16[128,768]{1,0:T(8,128)(2,1)}, u32[]{:S(2)}) copy-start(bf16[128,768]{1,0:T(8,128)(2,1)} %grad_hbm.1) | copy-start | bytes 589828
  2.5 0.7 %copy-start.2 = (s32[128,1]{0,1:T(1,128)S(1)}, s32[128,1]{0,1:T(1,128)}, u32[]{:S(2)}) copy-start(s32[128,1]{0,1:T(1,128)} %param.7) | copy-start | bytes 1540
  3.1 0.7 %copy-start.3 = (f32[128]{0:T(128)S(1)}, f32[128]{0:T(128)}, u32[]{:S(2)}) copy-start(f32[128]{0:T(128)} %param.8) | copy-start | bytes 1540

commit v5 on v3

--- a/solution.py
+++ b/solution.py
@@ -199,7 +199,7 @@
 
         @pl.loop(1, n)
         def _(k):
-            source = lax.rem(me + k, n)
+            source = lax.rem(me + n - k, n)
             wait_block(kind, src, dst, source)
             forward(kind, dst, source).start()
             then(k)

time: 54.1 us -> 54.5 us (level)
  no operation moved by 1% of the time
where the time goes in v5:
time: 54.5 us; the launch traced here: 53.9 us
  Pallas kernels  45.4 us (83%)
  local copies, waits for them, and re-layouts  7.83 us (14%)
  between operations  0.65 us (1%)
    pallas_call x1, Pallas kernels, local_fused(): pl.pallas_call(functools.partial(kernel, n, cap), out_shape=(jax.ShapeDty...  45.4 us
    unnamed x13, local copies, waits for them, and re-layouts  7.83 us

profile of v5, /device:TPU:28, one launch (start us, length us, event | category | flops | bytes accessed | tf_op | source)
XLA Modules:
  0.0 53.9 jit_solution(2734448378592183308)
XLA Ops:
  0.6 0.0 copy-start
  0.6 0.9 %copy-done = bf16[128,768]{1,0:T(8,128)(2,1)S(1)} copy-done((bf16[128,768]{1,0:T(8,128)(2,1)S(1)}, bf16[128,768]{1,0:T(8,128)(2,1)}, u32[]{:S(2)}) %copy-start) | copy-done | bytes 196632
  1.6 0.0 copy-start.1
  1.6 0.9 %copy-done.1 = bf16[128,768]{1,0:T(8,128)(2,1)S(1)} copy-done((bf16[128,768]{1,0:T(8,128)(2,1)S(1)}, bf16[128,768]{1,0:T(8,128)(2,1)}, u32[]{:S(2)}) %copy-start.1) | copy-done | bytes 196632
  2.5 0.0 copy-start.2
  2.5 0.7 %copy-done.2 = s32[128,1]{0,1:T(1,128)S(1)} copy-done((s32[128,1]{0,1:T(1,128)S(1)}, s32[128,1]{0,1:T(1,128)}, u32[]{:S(2)}) %copy-start.2) | copy-done | bytes 536
  3.1 0.0 copy-start.3
  3.1 0.7 %copy-done.3 = f32[128]{0:T(128)S(1)} copy-done((f32[128]{0:T(128)S(1)}, f32[128]{0:T(128)}, u32[]{:S(2)}) %copy-start.3) | copy-done | bytes 536
  3.8 45.4 %shard_map.101 = (bf16[128,768]{1,0:T(8,128)(2,1)S(1)}, bf16[128,768]{1,0:T(8,128)(2,1)S(1)}, f32[1,128]{1,0:T(1,128)S(1)}, bf16[1,768,1536]{2,1,0:T(8,128)(2,1)S(1)}, bf16[1,1536,768]{2,1,0:T(8,128)(2,1)S(1)}) custom-call(bf16[128,768]{1,0:T(8,128)(2,1)S(1)} %copy-done, s32[1,128]{1,0:T(1,128)S(1)} %bitcast.3, f32[1,128]{1,0:T(1,128)S(1)} %bitcast.4, ...), custom_call_target="tpu_custom_call" | custom-call | flops 7247757312 | bytes 9437184 | tf_op jit(solution)/shard_map/pallas_call | solution.py:387
  49.2 0.7 %copy.16 = bf16[128,768]{1,0:T(8,128)(2,1)} copy(bf16[128,768]{1,0:T(8,128)(2,1)S(1)} %get-tuple-element.20) | data formatting | bytes 393216
  49.9 0.7 %copy.17 = bf16[128,768]{1,0:T(8,128)(2,1)} copy(bf16[128,768]{1,0:T(8,128)(2,1)S(1)} %get-tuple-element.21) | data formatting | bytes 393216
  50.6 0.5 copy.18
  51.1 1.4 %copy.19 = bf16[1,768,1536]{2,1,0:T(8,128)(2,1)} copy(bf16[1,768,1536]{2,1,0:T(8,128)(2,1)S(1)} %get-tuple-element.23) | data formatting | bytes 4718592
  52.5 1.4 %copy.20 = bf16[1,1536,768]{2,1,0:T(8,128)(2,1)} copy(bf16[1,1536,768]{2,1,0:T(8,128)(2,1)S(1)} %get-tuple-element.24) | data formatting | bytes 4718592
Async XLA Ops:
  0.6 0.9 %copy-start = (bf16[128,768]{1,0:T(8,128)(2,1)S(1)}, bf16[128,768]{1,0:T(8,128)(2,1)}, u32[]{:S(2)}) copy-start(bf16[128,768]{1,0:T(8,128)(2,1)} %tok_hbm.1) | copy-start | bytes 589828
  1.6 0.9 %copy-start.1 = (bf16[128,768]{1,0:T(8,128)(2,1)S(1)}, bf16[128,768]{1,0:T(8,128)(2,1)}, u32[]{:S(2)}) copy-start(bf16[128,768]{1,0:T(8,128)(2,1)} %grad_hbm.1) | copy-start | bytes 589828
  2.5 0.7 %copy-start.2 = (s32[128,1]{0,1:T(1,128)S(1)}, s32[128,1]{0,1:T(1,128)}, u32[]{:S(2)}) copy-start(s32[128,1]{0,1:T(1,128)} %param.7) | copy-start | bytes 1540
  3.1 0.7 %copy-start.3 = (f32[128]{0:T(128)S(1)}, f32[128]{0:T(128)}, u32[]{:S(2)}) copy-start(f32[128]{0:T(128)} %param.8) | copy-start | bytes 1540
